TPU v7x, 512 devices: a whole 4x4x16 slice. The times are simulated.
512 devices in a mesh: agent: 16 (over x, y), dp: 32 (over z, core).
Axes of the slice: x: 4, y: 4, z: 16, core: 2. Of those that a mesh axis runs over, the one named last changes fastest.
Arguments:
- learn_obs: bfloat16 [16, 1024, 16, 3456], P('agent', 'dp'), may hold values from -6 to 6
- own_obs: bfloat16 [16, 1024, 3456], P('agent', 'dp'), may hold values from -6 to 6
- opp_obs: bfloat16 [16, 1024, 3456], P('agent', 'dp'), may hold values from -6 to 6
- opponent: int32 [16, 1024, 1], P('agent', 'dp'), may hold values from 0 to 15; in each aligned block of 32 rows (0 to 31, 32 to 63, ..., all dimensions but the last counted through in order) at most 8 rows name the same one
- actions: int32 [16, 1024, 16], P('agent', 'dp'), may hold values from 0 to 17
- done: int32 [16, 1024, 16], P('agent', 'dp'), may hold values 0 or 1
- rewards: float32 [16, 1024, 16], P('agent', 'dp'), may hold values from -6 to 6
- behaviour: float32 [16, 1024, 16], P('agent', 'dp'), may hold values from -4.5 to -1.5
- core_master: float32 [16, 256, 3712], P('agent', 'dp'), may hold values from -0.109375 to 0.109375
- core_mom: float32 [16, 256, 3712], P('agent', 'dp'), may hold values from -6 to 6
- core_vel: float32 [16, 256, 3712], P('agent', 'dp'), may hold values from 0.1 to 1
- head_master: float32 [16, 19, 256], P('agent'), may hold values from -0.375 to 0.375
- head_mom: float32 [16, 19, 256], P('agent'), may hold values from -6 to 6
- head_vel: float32 [16, 19, 256], P('agent'), may hold values from 0.1 to 1
- rates: float32 [16], P('agent'), may hold values from 0.01 to 0.1
Outputs:
- own_logits: float32 [16, 1024, 18], P('agent', 'dp')
- opp_logits: bfloat16 [16, 1024, 18], P('agent', 'dp')
- new_core: float32 [16, 256, 3712], P('agent', 'dp')
- new_core_mom: float32 [16, 256, 3712], P('agent', 'dp')
- new_core_vel: float32 [16, 256, 3712], P('agent', 'dp')
- new_head: float32 [16, 19, 256], P('agent')
- new_head_mom: float32 [16, 19, 256], P('agent')
- new_head_vel: float32 [16, 19, 256], P('agent')
Inputs may be any that keep to these rules, and one draw needn't show every extreme that they name: Among the 32 environments of one device (aligned blocks of the environment dimension), at most 8 face the same opponent agent, and some device reaches 8 in every draw.
All inputs are finite; a program needn't handle non-finite values. No bound on the sum of `done` on one device may be relied on, other than what follows from the above.
Results may differ from a plain program's by a relative error of at most 0.023.
Values may be sent and summed in bfloat16 or wider, within the bound.
A program may use at most 64 MiB of HBM per device.

v0:
```python
import jax
import jax.numpy as jnp
from jax import lax
from jax.sharding import Mesh
from jax.sharding import PartitionSpec as P

BLOCK = 128
DP = ("dp_0", "dp_1")
gamma_rate = 0.99
baseline_cost = 0.5
entropy_cost = 0.05
beta_first = 0.9
beta_second = 0.99
adam_eps = 1e-08


def joined_along(blocks, dim):
    shape = list(blocks.shape[1:])
    shape[dim] *= blocks.shape[0]
    return jnp.moveaxis(blocks, 0, dim).reshape(shape)


def stacked_from(x, axes, order):
    blocks = x[None]
    for k in order:
        blocks = lax.all_gather(blocks, axes[k], axis=0, tiled=True)
    current = [lax.axis_size(axes[k]) for k in reversed(order)]
    blocks = blocks.reshape(*current, *x.shape)
    turned = sorted(range(len(order)), key=lambda place: order[len(order) - 1 - place])
    return blocks.transpose(*turned, *range(len(order), blocks.ndim)).reshape(-1, *x.shape)


def gather_axes(x, axes, order, dim):
    return joined_along(stacked_from(x, axes, order), dim)


def reduced_to_own(blocks, axes, order):
    shape = [lax.axis_size(a) for a in axes]
    blocks = blocks.reshape(*shape, *blocks.shape[1:])
    blocks = blocks.transpose(*order, *range(len(axes), blocks.ndim))
    blocks = blocks.reshape(-1, *blocks.shape[len(axes) :])
    for k in order:
        blocks = lax.psum_scatter(blocks, axes[k], scatter_dimension=0, tiled=True)
    return blocks[0]


def in_blocks(x, dim, peers):
    before, after = (x.shape[:dim], x.shape[dim + 1 :])
    return jnp.moveaxis(x.reshape(*before, peers, -1, *after), dim, 0)


def sum_by_axis(x, axes, order, dim):
    peers = lax.axis_size(axes)
    return reduced_to_own(in_blocks(x, dim, peers), axes, order)


def by_axis(x, axes):
    for axis in axes:
        x = lax.psum(x, axis)
    return x


def contract(left, right):
    return lax.dot_general(
        left, right, (((1,), (1,)), ((), ())), preferred_element_type=jnp.float32
    )


def contract_rows(left, right):
    return lax.dot_general(
        left, right, (((0,), (0,)), ((), ())), preferred_element_type=jnp.float32
    )


def forward(inputs, core_bf, head_bf):
    width = inputs.shape[-1]
    pre_one = contract(inputs, core_bf[:, :width])
    first_act = jax.nn.relu(pre_one)
    first_bf = first_act.astype(jnp.bfloat16)
    pre_two = contract(first_bf, core_bf[:, width:])
    second_act = jax.nn.relu(pre_two) + first_act
    second_bf = second_act.astype(jnp.bfloat16)
    network_outputs = contract(second_bf, head_bf)
    return (network_outputs, pre_one, first_bf, pre_two, second_bf)


def importance_trace_gradients(
    network_outputs, bootstrap_value, actions, done, rewards, behaviour, scale_factor
):
    action_count = network_outputs.shape[-1] - 1
    logits = network_outputs[..., :action_count]
    values = network_outputs[..., action_count]
    totals = jnp.sum(jnp.exp(logits), -1)
    logp = logits - jnp.log(totals)[..., None]
    probs = jnp.exp(logp)
    chosen = (actions[..., None] == jnp.arange(action_count, dtype=jnp.int32)).astype(jnp.float32)
    logp_act = jnp.sum(logp * chosen, -1)
    ratio = jnp.minimum(1.0, jnp.exp(logp_act - behaviour))
    discount = gamma_rate * (1.0 - done.astype(jnp.float32))
    next_values = jnp.concatenate([values[:, 1:], bootstrap_value[:, None]], 1)
    deltas = ratio * (rewards + discount * next_values - values)

    def backstep(carry, item):
        delta, factor = item
        carry = delta + factor * carry
        return (carry, carry)

    start = jnp.zeros((values.shape[0],), jnp.float32)
    final_carry, corrections = lax.scan(
        backstep, start, (deltas.T, (discount * ratio).T), reverse=True
    )
    targets = values + corrections.T
    next_targets = jnp.concatenate([targets[:, 1:], bootstrap_value[:, None]], 1)
    advantage = ratio * (rewards + discount * next_targets - values)
    entropy = -jnp.sum(probs * logp, -1)
    grad_logits = scale_factor * (
        -advantage[..., None] * (chosen - probs)
        + entropy_cost * probs * (logp + entropy[..., None])
    )
    grad_value = scale_factor * (-baseline_cost * (targets - values))
    return jnp.concatenate([grad_logits, grad_value[..., None]], -1)


def adam_step(master, moment, second, grad, rate):
    moment = beta_first * moment + (1.0 - beta_first) * grad
    second = beta_second * second + (1.0 - beta_second) * grad * grad
    master = master - rate * moment / (jnp.sqrt(second) + adam_eps)
    return (master, moment, second)


def per_device(
    learn_obs,
    own_obs,
    opp_obs,
    opponent,
    actions,
    done,
    rewards,
    behaviour,
    core_master,
    core_mom,
    core_vel,
    head_master,
    head_mom,
    head_vel,
    rates,
):
    environment_total, rollout_length, width = (
        learn_obs.shape[1],
        learn_obs.shape[2],
        learn_obs.shape[3],
    )
    action_count = head_master.shape[1] - 1
    agent_count = lax.axis_size("agent")
    slots = min(environment_total, BLOCK // agent_count)
    scale_factor = 1.0 / rollout_length
    core_bf = gather_axes(core_master.astype(jnp.bfloat16), DP, (0, 1), 1)[0]
    head_bf = head_master[0].astype(jnp.bfloat16)
    own_out = forward(own_obs[0], core_bf, head_bf)[0]
    ids = opponent[0, :, 0]
    earlier = (ids[None, :] == ids[:, None]) & jnp.tril(jnp.ones((ids.shape[0],) * 2, bool), -1)
    ranks = jnp.sum(earlier.astype(jnp.int32), 1)
    position = ids * slots + ranks
    placing = (
        position[None, :] == jnp.arange(agent_count * slots, dtype=jnp.int32)[:, None]
    ).astype(jnp.bfloat16)
    outgoing = jnp.dot(placing, opp_obs[0], preferred_element_type=jnp.float32).astype(jnp.bfloat16)
    outgoing = outgoing.reshape(agent_count, slots, width)
    incoming = lax.all_to_all(outgoing, "agent", split_axis=0, concat_axis=0, tiled=True)
    count = incoming.shape[1]
    played = forward(incoming.reshape(agent_count * count, width), core_bf, head_bf)[0][
        :, :action_count
    ]
    played = played.astype(jnp.bfloat16).reshape(agent_count, count, action_count)
    returned = lax.all_to_all(played, "agent", split_axis=0, concat_axis=0, tiled=True)
    opp_logits = returned.reshape(agent_count * slots, action_count)[position]
    rows = learn_obs[0].reshape(environment_total * rollout_length, width)
    network_outputs, pre_one, first_bf, pre_two, second_bf = forward(rows, core_bf, head_bf)
    output_gradient = importance_trace_gradients(
        network_outputs.reshape(environment_total, rollout_length, action_count + 1),
        own_out[:, action_count],
        actions[0],
        done[0],
        rewards[0],
        behaviour[0],
        scale_factor,
    )
    grad_bf = output_gradient.reshape(environment_total * rollout_length, action_count + 1).astype(
        jnp.bfloat16
    )
    head_grad = contract_rows(grad_bf, second_bf)
    grad_second = jnp.dot(grad_bf, head_bf, preferred_element_type=jnp.float32)
    grad_pre_two = jnp.where(pre_two > 0, grad_second, 0.0).astype(jnp.bfloat16)
    grad_first = grad_second + jnp.dot(
        grad_pre_two, core_bf[:, width:], preferred_element_type=jnp.float32
    )
    grad_pre_one = jnp.where(pre_one > 0, grad_first, 0.0).astype(jnp.bfloat16)
    core_grad = sum_by_axis(
        jnp.concatenate(
            [contract_rows(grad_pre_one, rows), contract_rows(grad_pre_two, first_bf)], 1
        ).astype(jnp.bfloat16),
        DP,
        (1, 0),
        0,
    ).astype(jnp.float32)
    head_total = by_axis(head_grad, DP)
    rate = rates[0]
    new_core, new_core_mom, new_core_vel = adam_step(
        core_master[0], core_mom[0], core_vel[0], core_grad, rate
    )
    new_head, new_head_mom, new_head_vel = adam_step(
        head_master[0], head_mom[0], head_vel[0], head_total, rate
    )
    return (
        own_out[:, :action_count][None],
        opp_logits[None],
        new_core[None],
        new_core_mom[None],
        new_core_vel[None],
        new_head[None],
        new_head_mom[None],
        new_head_vel[None],
    )


def solution(mesh):
    torus = Mesh(mesh.devices.reshape(mesh.shape["agent"], 16, 2), ("agent", "dp_0", "dp_1"))
    return jax.shard_map(
        per_device,
        mesh=torus,
        in_specs=(
            P("agent", DP, None, None),
            P("agent", DP, None),
            P("agent", DP, None),
            P("agent", DP, None),
            P("agent", DP, None),
            P("agent", DP, None),
            P("agent", DP, None),
            P("agent", DP, None),
            P("agent", DP, None),
            P("agent", DP, None),
            P("agent", DP, None),
            P("agent", None, None),
            P("agent", None, None),
            P("agent", None, None),
            P("agent"),
        ),
        out_specs=(
            P("agent", DP, None),
            P("agent", DP, None),
            P("agent", DP, None),
            P("agent", DP, None),
            P("agent", DP, None),
            P("agent", None, None),
            P("agent", None, None),
            P("agent", None, None),
        ),
        check_vma=False,
    )
```

profile of v0, /device:TPU:1, one launch (start us, length us, event | category | flops | bytes accessed | tf_op | source)
XLA Modules:
  0.0 268.0 jit_solution(14837776084978435782)
XLA Ops:
  8.3 37.6 %all-gather = bf16[16,8,3712]{2,1,0:T(8,128)(2,1)} all-gather(bf16[1,8,3712]{2,1,0:T(8,128)(2,1)S(1)} %convert_element_type.71), channel_id=2, replica_groups=mesh['agent'=16,'dp_0'=16,'dp_1'=2] {'dp_0'}, dimensions={0}, use_global_device_ids=true | all-gather | bytes 1009664 | tf_op jit(solution)/shard_map/all_gather | solution.py:26
  46.8 1.4 convert_element_type.81
  48.1 22.9 %all-gather.4.cloned.1.call-done = bf16[32,8,3712]{2,1,0:T(8,128)(2,1)} async-done(((bf16[16,8,3712]{2,1,0:T(8,128)(2,1)}), bf16[32,8,3712]{2,1,0:T(8,128)(2,1)}) %all-gather.4.cloned.1.call-update) | async-done | bytes 1900560 | tf_op jit(solution)/shard_map/all_gather | solution.py:26
  71.0 1.7 copy.180
  75.3 1.8 fusion.26
  77.1 2.6 fusion.4
  80.5 2.0 add_convert_fusion
  84.2 2.3 fusion.33
  89.7 1.3 fusion.71
  91.6 40.4 %while.17 = (s32[]{:T(128)}, f32[32]{0:T(128)}, f32[16,32]{1,0:T(8,128)}, f32[16,32]{1,0:T(8,128)}, f32[16,32]{1,0:T(8,128)}, /*index=5*/s32[]{:T(128)}, s32[]{:T(128)}, s32[]{:T(128)}) while((s32[]{:T(128)}, f32[32]{0:T(128)}, f32[16,32]{1,0:T(8,128)}, f32[16,32]{1,0:T(8,128)}, f32[16,32]{1,0:T(8,128)}, /*index=5*/s32[]{:T(128)}, ...), condition=%wide.region_4.5_spmd.clone, body=%wide.region_3.4_spmd.clone.sunk | while | flops 100 | bytes 891 | solution.py:109
  133.4 1.4 copy.188
  134.7 1.4 concatenate.38
  138.1 1.3 fusion.70
  140.2 1.9 fusion.31
  142.1 1.6 copy.189
  144.8 2.1 convolution_convert_fusion.2
  147.0 1.9 fusion.14
  148.9 1.8 copy.193
  150.7 2.1 convolution_convert_fusion
  152.9 1.4 copy.194
  155.2 2.2 fusion.3
  157.4 5.6 %all-to-all-start = ((bf16[16,8,3456]{2,1,0:T(8,128)(2,1)}), bf16[16,8,3456]{2,1,0:T(8,128)(2,1)}, u32[]{:S(2)}, u32[]{:S(2)}) async-start(bf16[16,8,3456]{2,1,0:T(8,128)(2,1)} %fusion.3), calls=%async_computation | async-start | bytes 1769472 | tf_op jit(solution)/shard_map/all_to_all | solution.py:169
  163.0 12.6 %reduce-scatter.5.cloned.1.call-done = bf16[16,8,3712]{2,1,0:T(8,128)(2,1)} async-done(((bf16[32,8,3712]{2,1,0:T(8,128)(2,1)}), bf16[16,8,3712]{2,1,0:T(8,128)(2,1)}) %reduce-scatter.5.cloned.1.call-update) | async-done | bytes 950288 | tf_op jit(solution)/shard_map/reduce_scatter | solution.py:43
  176.9 3.1 %fusion.15 = f32[128,256]{1,0:T(8,128)} fusion(bf16[256,3712]{1,0:T(8,128)(2,1)} %bitcast.156, bf16[16,8,3456]{2,1,0:T(8,128)(2,1)} %all-to-all-done), kind=kOutput, calls=%fused_computation.22 | convolution fusion | flops 226525184 | bytes 2785280 | tf_op jit(solution)/shard_map/dot_general | solution.py:64
  180.0 2.0 fusion.20
  182.0 1.4 copy.181
  183.4 5.7 %all-to-all-start.1 = ((bf16[16,8,18]{2,1,0:T(8,128)(2,1)}), bf16[16,8,18]{2,1,0:T(8,128)(2,1)}, u32[]{:S(2)}, u32[]{:S(2)}) async-start(bf16[16,8,18]{2,1,0:T(8,128)(2,1)} %bitcast.164), calls=%async_computation.1 | async-start | bytes 65536 | tf_op jit(solution)/shard_map/all_to_all | solution.py:175
  189.2 1.7 fusion.56
  190.9 45.8 %psum.14 = f32[19,256]{1,0:T(8,128)} all-reduce(f32[19,256]{1,0:T(8,128)} %fusion.56), channel_id=1, replica_groups=mesh['agent'=16,'dp_0'=16,'dp_1'=2] {'dp_0'}, use_global_device_ids=true, to_apply=%region_8.9 | all-reduce | flops 4864 | bytes 38912 | tf_op jit(solution)/shard_map/psum | solution.py:59
  236.7 17.5 %psum.15 = f32[19,256]{1,0:T(8,128)} all-reduce(f32[19,256]{1,0:T(8,128)} %psum.14), channel_id=1, replica_groups=mesh['agent'=16,'dp_0'=16,'dp_1'=2] {'dp_1'}, use_global_device_ids=true, to_apply=%region_9.10 | all-reduce | flops 4864 | bytes 38912 | tf_op jit(solution)/shard_map/psum | solution.py:59
  257.5 1.5 gather_fusion
  259.7 1.8 divide_subtract_fusion
  (96 shorter events, 62.0 us)
Async XLA Ops:
  7.2 69.9 %copy-start = (bf16[1,32,16,3456]{3,2,1,0:T(8,128)(2,1)S(1)}, bf16[1,32,16,3456]{3,2,1,0:T(8,128)(2,1)}, u32[]{:S(2)}) copy-start(bf16[1,32,16,3456]{3,2,1,0:T(8,128)(2,1)} %param.17) | copy-start | bytes 10616836
  7.2 63.8 %all-gather.4.cloned.1.call-start = ((), (), s32[]{:S(2)}) async-start(), calls=%async_computation.5 | async-start | bytes 2850816 | tf_op jit(solution)/shard_map/all_gather | solution.py:26
  46.0 129.6 %reduce-scatter.5.cloned.1.call-start = ((), (), s32[]{:S(2)}) async-start(), calls=%async_computation.4 | async-start | bytes 2850816 | tf_op jit(solution)/shard_map/reduce_scatter | solution.py:43
  46.8 37.5 %copy-start.7 = (s32[32,16]{1,0:T(8,128)}, s32[32,16]{1,0:T(8,128)S(1)}, u32[]{:S(2)}) copy-start(s32[32,16]{1,0:T(8,128)S(1)} %copy.182) | copy-start | bytes 6148
  71.0 3.0 %copy-start.12 = (bf16[1,32,3456]{2,1,0:T(8,128)(2,1)S(1)}, bf16[1,32,3456]{2,1,0:T(8,128)(2,1)}, u32[]{:S(2)}) copy-start(bf16[1,32,3456]{2,1,0:T(8,128)(2,1)} %param.18) | copy-start | bytes 663556
  72.7 1.3 copy-start.4
  77.1 6.1 %copy-start.8 = (bf16[1,19,256]{2,0,1:T(2,128)(2,1)S(1)}, bf16[1,19,256]{2,0,1:T(2,128)(2,1)}, u32[]{:S(2)}) copy-start(bf16[1,19,256]{2,0,1:T(2,128)(2,1)} %convert_element_type.81) | copy-start | bytes 29188
  79.7 0.8 copy-start.1
  82.5 0.7 copy-start.5
  143.7 3.3 %copy-start.2 = (f32[512,256]{1,0:T(8,128)S(1)}, f32[512,256]{1,0:T(8,128)}, u32[]{:S(2)}) copy-start(f32[512,256]{1,0:T(8,128)} %copy-done.1) | copy-start | bytes 1572868
  143.7 3.3 %copy-start.3 = (f32[512,256]{1,0:T(8,128)S(1)}, f32[512,256]{1,0:T(8,128)}, u32[]{:S(2)}) copy-start(f32[512,256]{1,0:T(8,128)} %get-tuple-element.223) | copy-start | bytes 1572868
  150.7 2.1 copy-start.6
  154.3 0.7 copy-start.11
  157.4 19.5 %all-to-all-start = ((bf16[16,8,3456]{2,1,0:T(8,128)(2,1)}), bf16[16,8,3456]{2,1,0:T(8,128)(2,1)}, u32[]{:S(2)}, u32[]{:S(2)}) async-start(bf16[16,8,3456]{2,1,0:T(8,128)(2,1)} %fusion.3), calls=%async_computation | async-start | bytes 1769472 | tf_op jit(solution)/shard_map/all_to_all | solution.py:169
  163.0 96.7 %reduce-scatter.7.cloned.1.call-start = ((), (), s32[]{:S(2)}) async-start(), calls=%async_computation.6 | async-start | bytes 1009664
  175.6 13.5 %copy-start.10 = (bf16[512,1]{0,1:T(2,128)(2,1)S(1)}, bf16[512,1]{0,1:T(2,128)(2,1)}, u32[]{:S(2)}) copy-start(bf16[512,1]{0,1:T(2,128)(2,1)} %concatenate.38) | copy-start | bytes 3076
  176.9 78.1 %copy-start.9 = (f32[32,19]{0,1:T(8,128)S(1)}, f32[32,19]{0,1:T(8,128)}, u32[]{:S(2)}) copy-start(f32[32,19]{0,1:T(8,128)} %fusion.26) | copy-start | bytes 7300
  183.4 74.1 %all-to-all-start.1 = ((bf16[16,8,18]{2,1,0:T(8,128)(2,1)}), bf16[16,8,18]{2,1,0:T(8,128)(2,1)}, u32[]{:S(2)}, u32[]{:S(2)}) async-start(bf16[16,8,18]{2,1,0:T(8,128)(2,1)} %bitcast.164), calls=%async_computation.1 | async-start | bytes 65536 | tf_op jit(solution)/shard_map/all_to_all | solution.py:175
Sparse Core Ops, SparseCore 0:
  46.1 24.8 all-gather.3
  154.5 21.0 reduce-scatter.4
  178.7 60.5 reduce-scatter.6
where the time goes:
time: 271 us; the launch traced here: 268 us
  blocking collectives  101 us (37%)
  local copies, waits for them, and re-layouts  46.2 us (17%)
  waiting for transfers between devices  35.5 us (13%)
  other arithmetic  35.2 us (13%)
  matrix products  24.1 us (9%)
  between operations  14.6 us (5%)
  starting transfers between devices  11.4 us (4%)
    psum x2, blocking collectives, by_axis(): x = lax.psum(x, axis)  63.3 us
    all_gather x1, blocking collectives, stacked_from(): blocks = lax.all_gather(blocks, axes[k], axis=0, tiled=True)  37.6 us
    all_gather x1, waiting for transfers between devices, stacked_from(): blocks = lax.all_gather(blocks, axes[k], axis=0, tiled=True)  22.9 us
    dynamic_update_slice x16, local copies, waits for them, and re-layouts, importance_trace_gradients(): lax.scan(backstep, start, (deltas.T, (discount * ratio).T), reverse=True)  20.6 us
    add x16, other arithmetic, backstep(): carry = delta + factor * carry  19.8 us
    dot_general x7, matrix products, contract(): lax.dot_general(left, right, (((1,), (1,)), ((), ())), preferred_element_...  13 us
    reduce_scatter x1, waiting for transfers between devices, reduced_to_own(): blocks = lax.psum_scatter(blocks, axes[k], scatter_dimension=0, tiled=True)  12.6 us
    unnamed x32, local copies, waits for them, and re-layouts  7.75 us
  transfers between devices with their start and end apart: 5, of which 2 were waited for; matrix products, arithmetic and copies ran while one was open for 7% of the time, Pallas kernels for 0%

commit v1 on v0

--- a/solution.py
+++ b/solution.py
@@ -12,6 +12,28 @@
 beta_first = 0.9
 beta_second = 0.99
 adam_eps = 1e-08
+
+
+def cut_along(x, dim, size):
+    before, after = (x.shape[:dim], x.shape[dim + 1 :])
+    return jnp.moveaxis(x.reshape(*before, size, -1, *after), dim, 0)
+
+
+def joined_along_2(pieces, dim):
+    lengths = list(pieces.shape[1:])
+    lengths[dim] *= pieces.shape[0]
+    return jnp.moveaxis(pieces, 0, dim).reshape(lengths)
+
+
+def exchange_directly(array, axis, split_dim, concat_dim):
+    count, here = (lax.axis_size(axis), lax.axis_index(axis))
+    pieces = cut_along(array, split_dim, count)
+    done = [pieces[here]]
+    for hop in range(1, count):
+        sent = pieces[(here + hop) % count]
+        done.append(lax.ppermute(sent, axis, [(i, (i + hop) % count) for i in range(count)]))
+    pieces = jnp.stack(done)[(here - jnp.arange(count)) % count]
+    return joined_along_2(pieces, concat_dim)
 
 
 def joined_along(blocks, dim):
@@ -166,7 +188,7 @@
     ).astype(jnp.bfloat16)
     outgoing = jnp.dot(placing, opp_obs[0], preferred_element_type=jnp.float32).astype(jnp.bfloat16)
     outgoing = outgoing.reshape(agent_count, slots, width)
-    incoming = lax.all_to_all(outgoing, "agent", split_axis=0, concat_axis=0, tiled=True)
+    incoming = exchange_directly(outgoing, "agent", 0, 0)
     count = incoming.shape[1]
     played = forward(incoming.reshape(agent_count * count, width), core_bf, head_bf)[0][
         :, :action_count

time: 271 us -> 323 us (1.19)
  starting transfers between devices: 11.4 us -> 60.7 us
  local copies, waits for them, and re-layouts: 46.2 us -> 68.8 us
  waiting for transfers between devices: 35.5 us -> 15.3 us
    ppermute x0 -> x15, starting transfers between devices: none -> 54.8 us  [exchange_directly(): lax.ppermute(sent, axis, [(i, (i + hop) % count) for i in range(count)])]
    all_gather x1, waiting for transfers between devices: 22.9 us -> 0.01 us  [stacked_from(): blocks = lax.all_gather(blocks, axes[k], axis=0, tiled=True)]
    unnamed x32 -> x46, local copies, waits for them, and re-layouts: 7.75 us -> 24 us
    all_to_all x1 -> x0, starting transfers between devices: 5.58 us -> none  [per_device(): lax.all_to_all(outgoing, 'agent', split_axis=0, concat_axis=0, tiled=True)]
  transfers between devices with their start and end apart: 5 -> 19, of which waited for: 2 -> 1; matrix products, arithmetic and copies ran while one was open for 7% -> 38% of each run, Pallas kernels for 0% -> 0%
where the time goes in v1:
time: 323 us; the launch traced here: 319 us
  blocking collectives  100 us (31%)
  local copies, waits for them, and re-layouts  68.8 us (21%)
  starting transfers between devices  60.7 us (19%)
  other arithmetic  35.6 us (11%)
  matrix products  24.1 us (7%)
  waiting for transfers between devices  15.3 us (5%)
  between operations  14.9 us (5%)
    psum x2, blocking collectives, by_axis(): x = lax.psum(x, axis)  62.4 us
    ppermute x15, starting transfers between devices, exchange_directly(): lax.ppermute(sent, axis, [(i, (i + hop) % count) for i in range(count)])  54.8 us
    all_gather x1, blocking collectives, stacked_from(): blocks = lax.all_gather(blocks, axes[k], axis=0, tiled=True)  37.6 us
    unnamed x46, local copies, waits for them, and re-layouts  24 us
    dynamic_update_slice x16, local copies, waits for them, and re-layouts, importance_trace_gradients(): lax.scan(backstep, start, (deltas.T, (discount * ratio).T), reverse=True)  20.6 us
    add x16, other arithmetic, backstep(): carry = delta + factor * carry  19.6 us
    reduce_scatter x1, waiting for transfers between devices, reduced_to_own(): blocks = lax.psum_scatter(blocks, axes[k], scatter_dimension=0, tiled=True)  15.2 us
    dot_general x7, matrix products, contract(): lax.dot_general(left, right, (((1,), (1,)), ((), ())), preferred_element_...  12.9 us
  transfers between devices with their start and end apart: 19, of which 1 were waited for; matrix products, arithmetic and copies ran while one was open for 38% of the time, Pallas kernels for 0%

profile of v1, /device:TPU:1, one launch (start us, length us, event | category | flops | bytes accessed | tf_op | source)
XLA Modules:
  0.0 319.4 jit_solution(1464454853503037495)
XLA Ops:
  8.3 37.6 %all-gather = bf16[16,8,3712]{2,1,0:T(8,128)(2,1)} all-gather(bf16[1,8,3712]{2,1,0:T(8,128)(2,1)S(1)} %convert_element_type.71), channel_id=2, replica_groups=mesh['agent'=16,'dp_0'=16,'dp_1'=2] {'dp_0'}, dimensions={0}, use_global_device_ids=true | all-gather | bytes 1009664 | tf_op jit(solution)/shard_map/all_gather | solution.py:48
  46.4 2.2 fusion.3
  48.6 2.1 dynamic-slice_bitcast_fusion
  50.7 3.2 %collective-permute-start = (bf16[1,8,3456]{2,1,0:T(8,128)(2,1)}, bf16[1,8,3456]{2,1,0:T(8,128)(2,1)}, u32[]{:S(2)}, u32[]{:S(2)}) collective-permute-start(bf16[1,8,3456]{2,1,0:T(8,128)(2,1)} %get-tuple-element.227), channel_id=1, source_target_pairs={{0,32},{32,64},{64,96},{96,128},{128,160},{160,192},{192,224},{224... | collective-permute-start | bytes 165896 | tf_op jit(solution)/shard_map/ppermute | solution.py:34
  53.9 4.5 %collective-permute-start.1 = (bf16[1,8,3456]{2,1,0:T(8,128)(2,1)}, bf16[1,8,3456]{2,1,0:T(8,128)(2,1)}, u32[]{:S(2)}, u32[]{:S(2)}) collective-permute-start(bf16[1,8,3456]{2,1,0:T(8,128)(2,1)} %get-tuple-element.226), channel_id=1, source_target_pairs={{0,64},{32,96},{64,128},{96,160},{128,192},{160,224},{192,256},{22... | collective-permute-start | bytes 165896 | tf_op jit(solution)/shard_map/ppermute | solution.py:34
  58.5 3.9 %collective-permute-start.2 = (bf16[1,8,3456]{2,1,0:T(8,128)(2,1)}, bf16[1,8,3456]{2,1,0:T(8,128)(2,1)}, u32[]{:S(2)}, u32[]{:S(2)}) collective-permute-start(bf16[1,8,3456]{2,1,0:T(8,128)(2,1)} %get-tuple-element.225), channel_id=1, source_target_pairs={{0,96},{32,128},{64,160},{96,192},{128,224},{160,256},{192,288},{2... | collective-permute-start | bytes 165896 | tf_op jit(solution)/shard_map/ppermute | solution.py:34
  62.4 3.1 collective-permute-start.3
  65.5 2.9 collective-permute-start.4
  72.5 3.1 collective-permute-start.5
  77.0 4.8 %collective-permute-start.6 = (bf16[1,8,3456]{2,1,0:T(8,128)(2,1)}, bf16[1,8,3456]{2,1,0:T(8,128)(2,1)S(1)}, u32[]{:S(2)}, u32[]{:S(2)}) collective-permute-start(bf16[1,8,3456]{2,1,0:T(8,128)(2,1)} %get-tuple-element.221), channel_id=1, source_target_pairs={{0,224},{32,256},{64,288},{96,320},{128,352},{160,384},{192,416},{... | collective-permute-start | bytes 165896 | tf_op jit(solution)/shard_map/ppermute | solution.py:34
  83.3 3.6 %collective-permute-start.7 = (bf16[1,8,3456]{2,1,0:T(8,128)(2,1)}, bf16[1,8,3456]{2,1,0:T(8,128)(2,1)S(1)}, u32[]{:S(2)}, u32[]{:S(2)}) collective-permute-start(bf16[1,8,3456]{2,1,0:T(8,128)(2,1)} %get-tuple-element.220), channel_id=1, source_target_pairs={{0,256},{32,288},{64,320},{96,352},{128,384},{160,416},{192,448},{... | collective-permute-start | bytes 165896 | tf_op jit(solution)/shard_map/ppermute | solution.py:34
  88.4 3.5 %collective-permute-start.8 = (bf16[1,8,3456]{2,1,0:T(8,128)(2,1)}, bf16[1,8,3456]{2,1,0:T(8,128)(2,1)S(1)}, u32[]{:S(2)}, u32[]{:S(2)}) collective-permute-start(bf16[1,8,3456]{2,1,0:T(8,128)(2,1)} %get-tuple-element.219), channel_id=1, source_target_pairs={{0,288},{32,320},{64,352},{96,384},{128,416},{160,448},{192,480},{... | collective-permute-start | bytes 165896 | tf_op jit(solution)/shard_map/ppermute | solution.py:34
  93.4 5.3 %collective-permute-start.9 = (bf16[1,8,3456]{2,1,0:T(8,128)(2,1)}, bf16[1,8,3456]{2,1,0:T(8,128)(2,1)}, u32[]{:S(2)}, u32[]{:S(2)}) collective-permute-start(bf16[1,8,3456]{2,1,0:T(8,128)(2,1)} %get-tuple-element.218), channel_id=1, source_target_pairs={{0,320},{32,352},{64,384},{96,416},{128,448},{160,480},{192,0},{22... | collective-permute-start | bytes 165896 | tf_op jit(solution)/shard_map/ppermute | solution.py:34
  100.2 4.8 %collective-permute-start.10 = (bf16[1,8,3456]{2,1,0:T(8,128)(2,1)}, bf16[1,8,3456]{2,1,0:T(8,128)(2,1)}, u32[]{:S(2)}, u32[]{:S(2)}) collective-permute-start(bf16[1,8,3456]{2,1,0:T(8,128)(2,1)} %get-tuple-element.217), channel_id=1, source_target_pairs={{0,352},{32,384},{64,416},{96,448},{128,480},{160,0},{192,32},{224... | collective-permute-start | bytes 165896 | tf_op jit(solution)/shard_map/ppermute | solution.py:34
  105.6 3.8 %collective-permute-start.11 = (bf16[1,8,3456]{2,1,0:T(8,128)(2,1)}, bf16[1,8,3456]{2,1,0:T(8,128)(2,1)}, u32[]{:S(2)}, u32[]{:S(2)}) collective-permute-start(bf16[1,8,3456]{2,1,0:T(8,128)(2,1)} %get-tuple-element.216), channel_id=1, source_target_pairs={{0,384},{32,416},{64,448},{96,480},{128,0},{160,32},{192,64},{224,... | collective-permute-start | bytes 165896 | tf_op jit(solution)/shard_map/ppermute | solution.py:34
  110.0 1.9 collective-permute-start.12
  112.5 2.5 collective-permute-start.13
  121.7 2.6 fusion.4
  125.1 2.0 add_convert_fusion
  128.9 2.3 fusion.33
  136.3 40.2 %while.17 = (s32[]{:T(128)}, f32[32]{0:T(128)}, f32[16,32]{1,0:T(8,128)}, f32[16,32]{1,0:T(8,128)}, f32[16,32]{1,0:T(8,128)}, /*index=5*/s32[]{:T(128)}, s32[]{:T(128)}, s32[]{:T(128)}) while((s32[]{:T(128)}, f32[32]{0:T(128)}, f32[16,32]{1,0:T(8,128)}, f32[16,32]{1,0:T(8,128)}, f32[16,32]{1,0:T(8,128)}, /*index=5*/s32[]{:T(128)}, ...), condition=%wide.region_4.5_spmd.clone, body=%wide.region_3.4_spmd.clone.sunk | while | flops 100 | bytes 891 | solution.py:131
  184.6 1.9 fusion.31
  189.2 2.1 convolution_convert_fusion.2
  195.0 2.1 convolution_convert_fusion
  198.7 3.7 %collective-permute-start.14 = (bf16[1,8,3456]{2,1,0:T(8,128)(2,1)}, bf16[1,8,3456]{2,1,0:T(8,128)(2,1)}, u32[]{:S(2)}, u32[]{:S(2)}) collective-permute-start(bf16[1,8,3456]{2,1,0:T(8,128)(2,1)} %get-tuple-element.213), channel_id=1, source_target_pairs={{0,480},{32,0},{64,32},{96,64},{128,96},{160,128},{192,160},{224,1... | collective-permute-start | bytes 165896 | tf_op jit(solution)/shard_map/ppermute | solution.py:34
  209.7 15.2 %reduce-scatter.5.cloned.1.call-done = bf16[16,8,3712]{2,1,0:T(8,128)(2,1)} async-done(((bf16[32,8,3712]{2,1,0:T(8,128)(2,1)}), bf16[16,8,3712]{2,1,0:T(8,128)(2,1)}) %reduce-scatter.5.cloned.1.call-update) | async-done | bytes 950288 | tf_op jit(solution)/shard_map/reduce_scatter | solution.py:65
  226.3 2.9 gather_fusion
  229.2 3.1 fusion.15
  232.3 2.0 fusion.20
  235.7 5.7 %all-to-all-start = ((bf16[16,8,18]{2,1,0:T(8,128)(2,1)}), bf16[16,8,18]{2,1,0:T(8,128)(2,1)}, u32[]{:S(2)}, u32[]{:S(2)}) async-start(bf16[16,8,18]{2,1,0:T(8,128)(2,1)} %bitcast.228), calls=%async_computation | async-start | bytes 65536 | tf_op jit(solution)/shard_map/all_to_all | solution.py:197
  243.2 45.4 %psum.14 = f32[19,256]{1,0:T(8,128)} all-reduce(f32[19,256]{1,0:T(8,128)} %fusion.56), channel_id=1, replica_groups=mesh['agent'=16,'dp_0'=16,'dp_1'=2] {'dp_0'}, use_global_device_ids=true, to_apply=%region_8.9 | all-reduce | flops 4864 | bytes 38912 | tf_op jit(solution)/shard_map/psum | solution.py:81
  288.5 17.0 %psum.15 = f32[19,256]{1,0:T(8,128)} all-reduce(f32[19,256]{1,0:T(8,128)} %psum.14), channel_id=1, replica_groups=mesh['agent'=16,'dp_0'=16,'dp_1'=2] {'dp_1'}, use_global_device_ids=true, to_apply=%region_9.10 | all-reduce | flops 4864 | bytes 38912 | tf_op jit(solution)/shard_map/psum | solution.py:81
  (143 shorter events, 103.4 us)
Async XLA Ops:
  7.2 114.5 %copy-start = (bf16[1,32,16,3456]{3,2,1,0:T(8,128)(2,1)S(1)}, bf16[1,32,16,3456]{3,2,1,0:T(8,128)(2,1)}, u32[]{:S(2)}) copy-start(bf16[1,32,16,3456]{3,2,1,0:T(8,128)(2,1)} %param.17) | copy-start | bytes 10616836
  7.2 39.0 %copy-start.11 = (s32[1,32,1]{1,2,0:T(1,128)S(1)}, s32[1,32,1]{1,2,0:T(1,128)}, u32[]{:S(2)}) copy-start(s32[1,32,1]{1,2,0:T(1,128)} %param.20) | copy-start | bytes 388
  7.2 108.5 %all-gather.4.cloned.1.call-start = ((), (), s32[]{:S(2)}) async-start(), calls=%async_computation.4 | async-start | bytes 2850816 | tf_op jit(solution)/shard_map/all_gather | solution.py:48
  46.0 178.9 %reduce-scatter.5.cloned.1.call-start = ((), (), s32[]{:S(2)}) async-start(), calls=%async_computation.3 | async-start | bytes 2850816 | tf_op jit(solution)/shard_map/reduce_scatter | solution.py:65
  50.7 21.8 %collective-permute-start = (bf16[1,8,3456]{2,1,0:T(8,128)(2,1)}, bf16[1,8,3456]{2,1,0:T(8,128)(2,1)}, u32[]{:S(2)}, u32[]{:S(2)}) collective-permute-start(bf16[1,8,3456]{2,1,0:T(8,128)(2,1)} %get-tuple-element.227), channel_id=1, source_target_pairs={{0,32},{32,64},{64,96},{96,128},{128,160},{160,192},{192,224},{224... | collective-permute-start | bytes 165896 | tf_op jit(solution)/shard_map/ppermute | solution.py:34
  53.9 23.1 %collective-permute-start.1 = (bf16[1,8,3456]{2,1,0:T(8,128)(2,1)}, bf16[1,8,3456]{2,1,0:T(8,128)(2,1)}, u32[]{:S(2)}, u32[]{:S(2)}) collective-permute-start(bf16[1,8,3456]{2,1,0:T(8,128)(2,1)} %get-tuple-element.226), channel_id=1, source_target_pairs={{0,64},{32,96},{64,128},{96,160},{128,192},{160,224},{192,256},{22... | collective-permute-start | bytes 165896 | tf_op jit(solution)/shard_map/ppermute | solution.py:34
  58.5 24.8 %collective-permute-start.2 = (bf16[1,8,3456]{2,1,0:T(8,128)(2,1)}, bf16[1,8,3456]{2,1,0:T(8,128)(2,1)}, u32[]{:S(2)}, u32[]{:S(2)}) collective-permute-start(bf16[1,8,3456]{2,1,0:T(8,128)(2,1)} %get-tuple-element.225), channel_id=1, source_target_pairs={{0,96},{32,128},{64,160},{96,192},{128,224},{160,256},{192,288},{2... | collective-permute-start | bytes 165896 | tf_op jit(solution)/shard_map/ppermute | solution.py:34
  62.4 26.0 %collective-permute-start.3 = (bf16[1,8,3456]{2,1,0:T(8,128)(2,1)}, bf16[1,8,3456]{2,1,0:T(8,128)(2,1)}, u32[]{:S(2)}, u32[]{:S(2)}) collective-permute-start(bf16[1,8,3456]{2,1,0:T(8,128)(2,1)} %get-tuple-element.224), channel_id=1, source_target_pairs={{0,128},{32,160},{64,192},{96,224},{128,256},{160,288},{192,320},{... | collective-permute-start | bytes 165896 | tf_op jit(solution)/shard_map/ppermute | solution.py:34
  65.5 27.9 %collective-permute-start.4 = (bf16[1,8,3456]{2,1,0:T(8,128)(2,1)}, bf16[1,8,3456]{2,1,0:T(8,128)(2,1)}, u32[]{:S(2)}, u32[]{:S(2)}) collective-permute-start(bf16[1,8,3456]{2,1,0:T(8,128)(2,1)} %get-tuple-element.223), channel_id=1, source_target_pairs={{0,160},{32,192},{64,224},{96,256},{128,288},{160,320},{192,352},{... | collective-permute-start | bytes 165896 | tf_op jit(solution)/shard_map/ppermute | solution.py:34
  71.1 57.8 %copy-start.7 = (s32[32,16]{1,0:T(8,128)}, s32[32,16]{1,0:T(8,128)S(1)}, u32[]{:S(2)}) copy-start(s32[32,16]{1,0:T(8,128)S(1)} %copy.182) | copy-start | bytes 6148
  72.5 27.7 %collective-permute-start.5 = (bf16[1,8,3456]{2,1,0:T(8,128)(2,1)}, bf16[1,8,3456]{2,1,0:T(8,128)(2,1)S(1)}, u32[]{:S(2)}, u32[]{:S(2)}) collective-permute-start(bf16[1,8,3456]{2,1,0:T(8,128)(2,1)} %get-tuple-element.222), channel_id=1, source_target_pairs={{0,192},{32,224},{64,256},{96,288},{128,320},{160,352},{192,384},{... | collective-permute-start | bytes 165896 | tf_op jit(solution)/shard_map/ppermute | solution.py:34
  77.0 28.5 %collective-permute-start.6 = (bf16[1,8,3456]{2,1,0:T(8,128)(2,1)}, bf16[1,8,3456]{2,1,0:T(8,128)(2,1)S(1)}, u32[]{:S(2)}, u32[]{:S(2)}) collective-permute-start(bf16[1,8,3456]{2,1,0:T(8,128)(2,1)} %get-tuple-element.221), channel_id=1, source_target_pairs={{0,224},{32,256},{64,288},{96,320},{128,352},{160,384},{192,416},{... | collective-permute-start | bytes 165896 | tf_op jit(solution)/shard_map/ppermute | solution.py:34
  83.3 26.7 %collective-permute-start.7 = (bf16[1,8,3456]{2,1,0:T(8,128)(2,1)}, bf16[1,8,3456]{2,1,0:T(8,128)(2,1)S(1)}, u32[]{:S(2)}, u32[]{:S(2)}) collective-permute-start(bf16[1,8,3456]{2,1,0:T(8,128)(2,1)} %get-tuple-element.220), channel_id=1, source_target_pairs={{0,256},{32,288},{64,320},{96,352},{128,384},{160,416},{192,448},{... | collective-permute-start | bytes 165896 | tf_op jit(solution)/shard_map/ppermute | solution.py:34
  88.4 24.2 %collective-permute-start.8 = (bf16[1,8,3456]{2,1,0:T(8,128)(2,1)}, bf16[1,8,3456]{2,1,0:T(8,128)(2,1)S(1)}, u32[]{:S(2)}, u32[]{:S(2)}) collective-permute-start(bf16[1,8,3456]{2,1,0:T(8,128)(2,1)} %get-tuple-element.219), channel_id=1, source_target_pairs={{0,288},{32,320},{64,352},{96,384},{128,416},{160,448},{192,480},{... | collective-permute-start | bytes 165896 | tf_op jit(solution)/shard_map/ppermute | solution.py:34
  93.4 105.3 %collective-permute-start.9 = (bf16[1,8,3456]{2,1,0:T(8,128)(2,1)}, bf16[1,8,3456]{2,1,0:T(8,128)(2,1)}, u32[]{:S(2)}, u32[]{:S(2)}) collective-permute-start(bf16[1,8,3456]{2,1,0:T(8,128)(2,1)} %get-tuple-element.218), channel_id=1, source_target_pairs={{0,320},{32,352},{64,384},{96,416},{128,448},{160,480},{192,0},{22... | collective-permute-start | bytes 165896 | tf_op jit(solution)/shard_map/ppermute | solution.py:34
  100.2 103.8 %collective-permute-start.10 = (bf16[1,8,3456]{2,1,0:T(8,128)(2,1)}, bf16[1,8,3456]{2,1,0:T(8,128)(2,1)}, u32[]{:S(2)}, u32[]{:S(2)}) collective-permute-start(bf16[1,8,3456]{2,1,0:T(8,128)(2,1)} %get-tuple-element.217), channel_id=1, source_target_pairs={{0,352},{32,384},{64,416},{96,448},{128,480},{160,0},{192,32},{224... | collective-permute-start | bytes 165896 | tf_op jit(solution)/shard_map/ppermute | solution.py:34
  105.6 99.8 %collective-permute-start.11 = (bf16[1,8,3456]{2,1,0:T(8,128)(2,1)}, bf16[1,8,3456]{2,1,0:T(8,128)(2,1)}, u32[]{:S(2)}, u32[]{:S(2)}) collective-permute-start(bf16[1,8,3456]{2,1,0:T(8,128)(2,1)} %get-tuple-element.216), channel_id=1, source_target_pairs={{0,384},{32,416},{64,448},{96,480},{128,0},{160,32},{192,64},{224,... | collective-permute-start | bytes 165896 | tf_op jit(solution)/shard_map/ppermute | solution.py:34
  110.0 96.8 %collective-permute-start.12 = (bf16[1,8,3456]{2,1,0:T(8,128)(2,1)}, bf16[1,8,3456]{2,1,0:T(8,128)(2,1)}, u32[]{:S(2)}, u32[]{:S(2)}) collective-permute-start(bf16[1,8,3456]{2,1,0:T(8,128)(2,1)} %get-tuple-element.215), channel_id=1, source_target_pairs={{0,416},{32,448},{64,480},{96,0},{128,32},{160,64},{192,96},{224,1... | collective-permute-start | bytes 165896 | tf_op jit(solution)/shard_map/ppermute | solution.py:34
  112.5 95.7 %collective-permute-start.13 = (bf16[1,8,3456]{2,1,0:T(8,128)(2,1)}, bf16[1,8,3456]{2,1,0:T(8,128)(2,1)}, u32[]{:S(2)}, u32[]{:S(2)}) collective-permute-start(bf16[1,8,3456]{2,1,0:T(8,128)(2,1)} %get-tuple-element.214), channel_id=1, source_target_pairs={{0,448},{32,480},{64,0},{96,32},{128,64},{160,96},{192,128},{224,1... | collective-permute-start | bytes 165896 | tf_op jit(solution)/shard_map/ppermute | solution.py:34
  115.7 3.0 copy-start.12
  117.4 1.3 copy-start.4
  121.7 6.1 %copy-start.8 = (bf16[1,19,256]{2,0,1:T(2,128)(2,1)S(1)}, bf16[1,19,256]{2,0,1:T(2,128)(2,1)}, u32[]{:S(2)}) copy-start(bf16[1,19,256]{2,0,1:T(2,128)(2,1)} %convert_element_type.81) | copy-start | bytes 29188
  124.3 0.8 copy-start.1
  127.1 0.7 copy-start.5
  188.1 3.2 %copy-start.2 = (f32[512,256]{1,0:T(8,128)S(1)}, f32[512,256]{1,0:T(8,128)}, u32[]{:S(2)}) copy-start(f32[512,256]{1,0:T(8,128)} %copy-done.1) | copy-start | bytes 1572868
  188.1 3.2 %copy-start.3 = (f32[512,256]{1,0:T(8,128)S(1)}, f32[512,256]{1,0:T(8,128)}, u32[]{:S(2)}) copy-start(f32[512,256]{1,0:T(8,128)} %get-tuple-element.239) | copy-start | bytes 1572868
  195.0 2.1 copy-start.6
  198.7 112.4 %reduce-scatter.7.cloned.1.call-start = ((), (), s32[]{:S(2)}) async-start(), calls=%async_computation.5 | async-start | bytes 1009664
  198.7 26.1 %collective-permute-start.14 = (bf16[1,8,3456]{2,1,0:T(8,128)(2,1)}, bf16[1,8,3456]{2,1,0:T(8,128)(2,1)}, u32[]{:S(2)}, u32[]{:S(2)}) collective-permute-start(bf16[1,8,3456]{2,1,0:T(8,128)(2,1)} %get-tuple-element.213), channel_id=1, source_target_pairs={{0,480},{32,0},{64,32},{96,64},{128,96},{160,128},{192,160},{224,1... | collective-permute-start | bytes 165896 | tf_op jit(solution)/shard_map/ppermute | solution.py:34
  229.2 12.2 %copy-start.10 = (bf16[512,1]{0,1:T(2,128)(2,1)S(1)}, bf16[512,1]{0,1:T(2,128)(2,1)}, u32[]{:S(2)}) copy-start(bf16[512,1]{0,1:T(2,128)(2,1)} %concatenate.38) | copy-start | bytes 3076
  229.2 77.2 %copy-start.9 = (f32[32,19]{0,1:T(8,128)S(1)}, f32[32,19]{0,1:T(8,128)}, u32[]{:S(2)}) copy-start(f32[32,19]{0,1:T(8,128)} %fusion.26) | copy-start | bytes 7300
  235.7 73.2 %all-to-all-start = ((bf16[16,8,18]{2,1,0:T(8,128)(2,1)}), bf16[16,8,18]{2,1,0:T(8,128)(2,1)}, u32[]{:S(2)}, u32[]{:S(2)}) async-start(bf16[16,8,18]{2,1,0:T(8,128)(2,1)} %bitcast.228), calls=%async_computation | async-start | bytes 65536 | tf_op jit(solution)/shard_map/all_to_all | solution.py:197
Sparse Core Ops, SparseCore 0:
  46.1 24.8 all-gather.3
  198.8 26.0 reduce-scatter.4
  227.9 61.1 reduce-scatter.6
